TPU v7x, 32 devices: a whole 2x2x4 slice. The times are simulated.
32 devices in a mesh: section: 4 (over x, core), tp: 4 (over z), cfg: 2 (over y).
Axes of the slice: x: 2, y: 2, z: 4, core: 2. Of those that a mesh axis runs over, the one named last changes fastest.
Arguments:
- inflow: bfloat16 [4, 512, 3072], P('section', 'cfg', 'tp'), parts along dimension 1, may hold values from -6 to 6
- w_qkv: bfloat16 [4, 3072, 3, 2048], P('section', None, None, 'tp'), may hold values from -0.109375 to 0.109375
- w_out: bfloat16 [4, 2048, 3072], P('section', 'tp'), may hold values from -0.125 to 0.125
- mod_shift: float32 [4, 3072], P('section'), may hold values from -3 to 3
- mod_scale: float32 [4, 3072], P('section'), may hold values from -1.5 to 1.5
- mod_gate: float32 [4, 3072], P('section'), may hold values from 0.5 to 1.5
- q_gain: float32 [4, 128], P('section'), may hold values from 1.5 to 4
- k_gain: float32 [4, 128], P('section'), may hold values from 0.5 to 1.5
- kv_cache: bfloat16 [4, 2048, 2, 2048], P('section', 'cfg', None, 'tp'), parts along dimension 1, may hold values from -6 to 6
- patch_id: int32 [2, 4], replicated, may hold values from 0 to 3, as said below
- positions: int32 [4, 256], replicated, may hold values from 0 to 1023, as said below
Outputs:
- outflow: bfloat16 [4, 512, 3072], P('section', 'cfg', 'tp'), parts along dimension 1
There are 2 independent parts, one for each index of `cfg`. A program takes and returns all parts, laid end to end along the dimension named above; an argument that names none is the same for every part. Nothing has to cross between parts.
Inputs may be any that keep to these rules, and one draw needn't show every extreme that they name: patch_id[t, s] = patch_id[t - 1, s - 1] with s - 1 taken modulo 4; each row names every patch once. `positions`: every token position stands exactly once.
All inputs are finite; a program needn't handle non-finite values.
Results may differ from a plain program's by a relative error of at most 0.015.
Values may be sent and summed in bfloat16 or wider, within the bound.
A program may use at most 128 MiB of HBM per device.

v0:
```python
import jax
import jax.numpy as jnp
from jax import lax
from jax.sharding import PartitionSpec as P

HD = 128
TICKS = 2


def passed_along(value, axis, steps):
    count = lax.axis_size(axis)
    pairs = [(source, (source + steps) % count) for source in range(count)]
    return lax.ppermute(value, axis, pairs)


def rms_scale(values, gain):
    moment = jnp.mean(values * values, axis=-1, keepdims=True)
    return values * lax.rsqrt(moment + 1e-06) * gain


def spread_rows(own_share):
    return lax.all_gather(own_share, "tp", axis=1, tiled=True)


def local(
    inflow,
    w_qkv,
    w_out,
    mod_shift,
    mod_scale,
    mod_gate,
    q_gain,
    k_gain,
    kv_cache,
    patch_id,
    positions,
):
    groups = lax.axis_size("tp")
    tp_rank = lax.axis_index("tp")
    section_no = lax.axis_index("section")
    width = w_out.shape[2]
    share_w = width // groups
    head_cols = w_out.shape[1]
    head_count = head_cols // HD
    tokens_all = kv_cache.shape[1]
    patch_rows = inflow.shape[1]
    weight_in = w_qkv[0].reshape(width, 3 * head_cols)
    weight_out = w_out[0]
    shift_v = mod_shift[0]
    scale_v = mod_scale[0]
    gate_v = mod_gate[0]
    start_col = tp_rank * share_w
    cache_raw = kv_cache[0]
    cache_keys = rms_scale(
        cache_raw[:, 0].astype(jnp.float32).reshape(tokens_all, head_count, HD), k_gain[0]
    ).astype(jnp.bfloat16)
    cache_vals = cache_raw[:, 1].reshape(tokens_all, head_count, HD)
    token_line = jnp.arange(tokens_all, dtype=jnp.int32)
    keep_mask = jnp.ones((tokens_all,), jnp.float32)
    fresh_keys = []
    fresh_vals = []
    own_share = inflow[0]
    gathered = spread_rows(own_share)
    outflow = own_share
    for tick_no in range(TICKS):
        patch_no = lax.dynamic_index_in_dim(patch_id[tick_no], section_no, 0, keepdims=False)
        rows_at = lax.dynamic_index_in_dim(positions, patch_no, 0, keepdims=False)
        state_f = gathered.astype(jnp.float32)
        center = jnp.mean(state_f, axis=-1, keepdims=True)
        varied = jnp.mean((state_f - center) * (state_f - center), axis=-1, keepdims=True)
        normed = (
            (state_f - center) * lax.rsqrt(varied + 1e-06) * (1.0 + scale_v) + shift_v
        ).astype(jnp.bfloat16)
        fresh = jnp.dot(normed, weight_in, preferred_element_type=jnp.float32)
        fresh = fresh.astype(jnp.bfloat16).reshape(patch_rows, 3, head_cols)
        queries = rms_scale(
            fresh[:, 0].astype(jnp.float32).reshape(patch_rows, head_count, HD), q_gain[0]
        ).astype(jnp.bfloat16)
        new_keys = rms_scale(
            fresh[:, 1].astype(jnp.float32).reshape(patch_rows, head_count, HD), k_gain[0]
        ).astype(jnp.bfloat16)
        fresh_keys.append(new_keys)
        fresh_vals.append(fresh[:, 2].reshape(patch_rows, head_count, HD))
        replaced = jnp.any(rows_at[:, None] == token_line[None, :], axis=0)
        keep_mask = keep_mask * (1.0 - replaced.astype(jnp.float32))
        scores = jnp.einsum(
            "phd,thd->hpt", queries, cache_keys, preferred_element_type=jnp.float32
        ) * HD ** (-0.5)
        expon = jnp.exp(scores) * keep_mask[None, None, :]
        total = jnp.sum(expon, axis=-1, keepdims=True)
        fresh_expon = []
        for block_keys in fresh_keys:
            block_scores = jnp.einsum(
                "phd,thd->hpt", queries, block_keys, preferred_element_type=jnp.float32
            ) * HD ** (-0.5)
            block_expon = jnp.exp(block_scores)
            total = total + jnp.sum(block_expon, axis=-1, keepdims=True)
            fresh_expon.append(block_expon)
        attn_probs = (expon / total).astype(jnp.bfloat16)
        mixed = jnp.einsum(
            "hpt,thd->phd", attn_probs, cache_vals, preferred_element_type=jnp.float32
        )
        for block_expon, block_vals in zip(fresh_expon, fresh_vals):
            block_probs = (block_expon / total).astype(jnp.bfloat16)
            mixed = mixed + jnp.einsum(
                "hpt,thd->phd", block_probs, block_vals, preferred_element_type=jnp.float32
            )
        mixed = mixed.astype(jnp.bfloat16).reshape(patch_rows, head_cols)
        partial_value = jnp.dot(mixed, weight_out, preferred_element_type=jnp.float32)
        summed = lax.psum(partial_value.astype(jnp.bfloat16), "tp").astype(jnp.float32)
        result = (state_f + gate_v * summed).astype(jnp.bfloat16)
        if tick_no + 1 < TICKS:
            gathered = passed_along(result, "section", 1)
        else:
            outflow = lax.dynamic_slice_in_dim(result, start_col, share_w, 1)
    return outflow[None]


def solution(mesh):
    placed = (
        P("section", "cfg", "tp"),
        P("section", None, None, "tp"),
        P("section", "tp", None),
        P("section", None),
        P("section", None),
        P("section", None),
        P("section", None),
        P("section", None),
        P("section", "cfg", None, "tp"),
        P(),
        P(),
    )
    return jax.shard_map(
        local, mesh=mesh, in_specs=placed, out_specs=P("section", "cfg", "tp"), check_vma=False
    )
```

profile of v0, /device:TPU:0, one launch (start us, length us, event | category | flops | bytes accessed | tf_op | source)
XLA Modules:
  0.0 255.7 jit_solution(767962411965226349)
XLA Ops:
  6.5 0.7 all-gather.3.cloned.1.call-update
  7.3 6.9 %slice_convert_fusion = (f32[1024,1,512]{2,1,0:T(1,128)}, bf16[1024,1,512]{2,1,0:T(2,128)(2,1)}) fusion(bf16[1024,2,512]{2,1,0:T(2,128)(2,1)} %bitcast.88), kind=kLoop, calls=%fused_computation.26 | loop fusion | flops 524288 | bytes 5242880 | tf_op jit(solution)/shard_map/convert_element_type | solution.py:55
  14.2 0.7 constant_dynamic-slice_fusion.1
  17.5 5.9 %copy.77 = bf16[1024,1,512]{0,2,1:T(8,128)(2,1)} copy(bf16[1024,1,512]{2,1,0:T(2,128)(2,1)} %get-tuple-element.6) | data formatting | bytes 2097152 | tf_op jit(solution)/shard_map/slice | solution.py:57
  23.3 12.7 %copy.69 = bf16[1,3072,3,512]{1,3,2,0:T(8,128)(2,1)} copy(bf16[1,3072,3,512]{3,1,2,0:T(8,128)(2,1)} %param.12) | data formatting | bytes 18874368 | tf_op args[1]
  37.8 2.9 %multiply_reduce_fusion.1 = f32[1024,4]{1,0:T(8,128)S(1)} fusion(f32[1024,4,128]{2,1,0:T(4,128)} %bitcast.84), kind=kLoop, calls=%fused_computation.28 | loop fusion | flops 1044480 | bytes 2113536 | tf_op jit(solution)/shard_map/reduce_sum | solution.py:17
  40.8 3.2 %multiply_convert_fusion = bf16[1024,4,128]{2,1,0:T(4,128)(2,1)} fusion(f32[1024,4,128]{2,1,0:T(4,128)S(1)} %bitcast.85, f32[128]{0:T(128)S(1)} %bitcast.121, f32[1024,4]{1,0:T(8,128)S(1)} %add_rsqrt_fusion), kind=kLoop, calls=%fused_computation.27 | loop fusion | flops 1572864 | bytes 3162624 | tf_op jit(solution)/shard_map/convert_element_type | solution.py:56
  44.0 4.7 %all-gather.3.cloned.1.call-done = bf16[1,256,3072]{2,1,0:T(8,128)(2,1)} async-done(((bf16[1,256,768]{2,1,0:T(8,128)(2,1)}), bf16[1,256,3072]{2,1,0:T(8,128)(2,1)}) %all-gather.3.cloned.1.call-update) | async-done | bytes 1572880 | tf_op jit(solution)/shard_map/all_gather | solution.py:22
  48.8 1.8 convert_reduce_fusion
  50.6 2.0 fusion.6
  52.6 7.3 %convolution_convert_fusion.3 = bf16[256,1536]{1,0:T(8,128)(2,1)} fusion(bf16[3072,1536]{0,1:T(8,128)(2,1)} %bitcast.86, bf16[1,256,3072]{2,1,0:T(8,128)(2,1)S(1)} %copy-done.3, f32[3072]{0:T(1024)S(1)} %bitcast.125, f32[3072]{0:T(1024)S(1)} %bitcast.112, f32[256]{0:T(256)S(1)} %add_rsqrt_fusion.6, f32[256]{0:T(256)S(1)} %broadcast_multiply_fusion.1), kind=kOutput, calls=%fused_computation.24 | convolution fusion | flops 2421030912 | bytes 11823104 | tf_op jit(solution)/shard_map/dot_general | solution.py:74
  59.9 2.3 copy.70
  62.2 1.2 fusion.70
  64.1 1.3 fusion.4
  65.4 1.1 fusion.28
  66.8 2.2 convolution_convert_fusion.1
  69.0 68.1 %all-reduce.3.cloned.1.call-done = bf16[256,3072]{1,0:T(8,128)(2,1)} async-done(((bf16[256,3072]{1,0:T(8,128)(2,1)}), bf16[256,3072]{1,0:T(8,128)(2,1)}) %all-reduce.3.cloned.1.call-update) | async-done | bytes 1572880 | tf_op jit(solution)/shard_map/psum | solution.py:110
  137.1 2.5 fusion.10
  139.9 19.8 %collective-permute-done = bf16[256,3072]{1,0:T(8,128)(2,1)S(1)} collective-permute-done((bf16[256,3072]{1,0:T(8,128)(2,1)S(1)}, bf16[256,3072]{1,0:T(8,128)(2,1)S(1)}, u32[]{:S(2)}, u32[]{:S(2)}) %collective-permute-start) | collective-permute-done | bytes 1572896 | tf_op jit(solution)/shard_map/ppermute | solution.py:13
  160.0 0.6 multiply_reduce_fusion
  160.9 7.3 %convolution_convert_fusion.2 = bf16[256,1536]{1,0:T(8,128)(2,1)} fusion(bf16[3072,1536]{0,1:T(8,128)(2,1)} %bitcast.87, bf16[256,3072]{1,0:T(8,128)(2,1)S(1)} %collective-permute-done, f32[256]{0:T(256)S(1)} %add_rsqrt_fusion.5, f32[256]{0:T(256)S(1)} %broadcast_multiply_fusion, f32[3072]{0:T(1024)S(1)} %bitcast.126, f32[3072]{0:T(1024)S(1)} %bitcast.113), kind=kOutput, calls=%fused_computation.23 | convolution fusion | flops 2421030912 | bytes 11823104 | tf_op jit(solution)/shard_map/dot_general | solution.py:74
  168.2 2.3 copy.79
  170.5 1.2 fusion.69
  171.9 0.5 fusion.74
  172.4 0.5 fusion.73
  172.8 1.3 fusion.5
  174.2 1.1 fusion.27
  175.5 0.7 copy-done.9
  176.5 2.2 convolution_convert_fusion
  178.8 3.5 %convert_element_type.163 = f32[256,3072]{1,0:T(8,128)} convert(bf16[256,3072]{1,0:T(8,128)(2,1)} %copy-done.2) | non-fusion elementwise | flops 786432 | bytes 4718592 | tf_op jit(solution)/shard_map/convert_element_type | solution.py:68
  182.3 64.8 %all-reduce.5.cloned.1.call-done = bf16[256,3072]{1,0:T(8,128)(2,1)} async-done(((bf16[256,3072]{1,0:T(8,128)(2,1)}), bf16[256,3072]{1,0:T(8,128)(2,1)}) %all-reduce.5.cloned.1.call-update) | async-done | bytes 1572880 | tf_op jit(solution)/shard_map/psum | solution.py:110
  247.1 2.1 fusion.56
  (65 shorter events, 3.2 us)
Async XLA Ops:
  6.5 60.2 %copy-start = (bf16[1,512,3072]{2,1,0:T(8,128)(2,1)S(1)}, bf16[1,512,3072]{2,1,0:T(8,128)(2,1)}, u32[]{:S(2)}) copy-start(bf16[1,512,3072]{2,1,0:T(8,128)(2,1)} %param.13) | copy-start | bytes 9437188
  6.5 42.2 %all-gather.3.cloned.1.call-start = ((), (), s32[]{:S(2)}) async-start(), calls=%async_computation.2 | async-start | bytes 1966080 | tf_op jit(solution)/shard_map/all_gather | solution.py:22
  7.3 129.9 %all-reduce.3.cloned.1.call-start = ((), (), s32[]{:S(2)}) async-start(), calls=%async_computation | async-start | bytes 3145728 | tf_op jit(solution)/shard_map/psum | solution.py:110
  7.3 6.9 %copy-start.14 = (s32[2,4]{1,0:T(2,128)S(1)}, s32[2,4]{1,0:T(2,128)}, u32[]{:S(2)}) copy-start(s32[2,4]{1,0:T(2,128)} %param.20) | copy-start | bytes 100
  23.3 14.0 %copy-start.13 = (s32[4,256]{1,0:T(4,128)S(1)}, s32[4,256]{1,0:T(4,128)}, u32[]{:S(2)}) copy-start(s32[4,256]{1,0:T(4,128)} %param.21) | copy-start | bytes 12292
  36.0 4.8 %copy-start.15 = (f32[1,128]{1,0:T(1,128)S(1)}, f32[1,128]{1,0:T(1,128)}, u32[]{:S(2)}) copy-start(f32[1,128]{1,0:T(1,128)} %param.18) | copy-start | bytes 1540
  37.3 3.5 %copy-start.1 = (f32[1024,1,512]{2,1,0:T(1,128)S(1)}, f32[1024,1,512]{2,1,0:T(1,128)}, u32[]{:S(2)}) copy-start(f32[1024,1,512]{2,1,0:T(1,128)} %get-tuple-element.5) | copy-start | bytes 6291460
  37.8 6.2 %copy-start.11 = (f32[1,3072]{1,0:T(1,128)S(1)}, f32[1,3072]{1,0:T(1,128)}, u32[]{:S(2)}) copy-start(f32[1,3072]{1,0:T(1,128)} %param.15) | copy-start | bytes 36868
  40.8 11.7 %copy-start.16 = (f32[1,3072]{1,0:T(1,128)S(1)}, f32[1,3072]{1,0:T(1,128)}, u32[]{:S(2)}) copy-start(f32[1,3072]{1,0:T(1,128)} %param.14) | copy-start | bytes 36868
  48.8 3.8 %copy-start.3 = (bf16[1,256,3072]{2,1,0:T(8,128)(2,1)S(1)}, bf16[1,256,3072]{2,1,0:T(8,128)(2,1)}, u32[]{:S(2)}) copy-start(bf16[1,256,3072]{2,1,0:T(8,128)(2,1)} %all-gather.3.cloned.1.call-done) | copy-start | bytes 4718596
  59.9 3.7 %copy-start.12 = (f32[1,128]{1,0:T(1,128)S(1)}, f32[1,128]{1,0:T(1,128)}, u32[]{:S(2)}) copy-start(f32[1,128]{1,0:T(1,128)} %param.17) | copy-start | bytes 1540
  62.2 1.9 copy-start.4
  63.4 3.1 %copy-start.8 = (bf16[256,1,512]{0,2,1:T(8,128)(2,1)}, bf16[256,1,512]{0,2,1:T(8,128)(2,1)S(1)}, u32[]{:S(2)}) copy-start(bf16[256,1,512]{0,2,1:T(8,128)(2,1)S(1)} %get-tuple-element.10) | copy-start | bytes 786436
  64.1 1.3 copy-start.6
  66.8 70.4 %copy-start.10 = (f32[1,3072]{1,0:T(1,128)S(1)}, f32[1,3072]{1,0:T(1,128)}, u32[]{:S(2)}) copy-start(f32[1,3072]{1,0:T(1,128)} %param.16) | copy-start | bytes 36868
  69.0 178.1 %all-reduce.5.cloned.1.call-start = ((), (), s32[]{:S(2)}) async-start(), calls=%async_computation.1 | async-start | bytes 3145728 | tf_op jit(solution)/shard_map/psum | solution.py:110
  139.6 20.1 %collective-permute-start = (bf16[256,3072]{1,0:T(8,128)(2,1)S(1)}, bf16[256,3072]{1,0:T(8,128)(2,1)S(1)}, u32[]{:S(2)}, u32[]{:S(2)}) collective-permute-start(bf16[256,3072]{1,0:T(8,128)(2,1)S(1)} %fusion.10), channel_id=1, source_target_pairs={{0,8},{8,16},{16,24},{24,0},{1,9},{9,17},{17,25},{25,1},{2,10},{10... | collective-permute-start | bytes 4718600 | tf_op jit(solution)/shard_map/ppermute | solution.py:13
  159.7 1.2 copy-start.2
  170.5 2.3 copy-start.5
  172.8 1.3 copy-start.7
  175.3 1.0 copy-start.9
Sparse Core Ops, SparseCore 0:
  8.9 39.7 all-gather.2
  69.1 67.9 all-reduce.2
  178.9 68.1 all-reduce.4
where the time goes:
time: 257 us; the launch traced here: 256 us
  waiting for transfers between devices  158 us (61%)
  local copies, waits for them, and re-layouts  27.4 us (11%)
  other arithmetic  26.5 us (10%)
  matrix products  25.9 us (10%)
  between operations  17.3 us (7%)
    psum x2, waiting for transfers between devices, local(): lax.psum(partial_value.astype(jnp.bfloat16), 'tp').astype(jnp.float32)  133 us
    ppermute x1, waiting for transfers between devices, passed_along(): return lax.ppermute(value, axis, pairs)  19.8 us
    dot_general x2, matrix products, local(): fresh = jnp.dot(normed, weight_in, preferred_element_type=jnp.float32)  14.6 us
    unnamed x35, local copies, waits for them, and re-layouts  13.7 us
    convert_element_type x1, other arithmetic, local(): cache_raw[:, 0].astype(jnp.float32).reshape(tokens_all, head_count, HD)  6.92 us
    slice x1, local copies, waits for them, and re-layouts, local(): cache_vals = cache_raw[:, 1].reshape(tokens_all, head_count, HD)  5.86 us
  transfers between devices with their start and end apart: 4, of which 4 were waited for; matrix products, arithmetic and copies ran while one was open for 14% of the time, Pallas kernels for 0%

commit v1 on v0

v1 whole, which is shorter than its diff:
```python
import functools

import jax
import jax.numpy as jnp
from jax import lax
from jax.experimental import pallas as pl
from jax.experimental.pallas import tpu as pltpu
from jax.sharding import PartitionSpec as P

HD = 128
TICKS = 2
CHUNKS = 4
MESH = pl.DeviceIdType.MESH
F32 = jnp.float32
BF16 = jnp.bfloat16


def head_norm(values, gain):
    moment = jnp.mean(values * values, axis=-1, keepdims=True)
    return (values * lax.rsqrt(moment + 1e-06) * gain).astype(BF16)


def kernel(
    n,
    sections,
    x_ref,
    wq_hbm,
    wo_hbm,
    shift_ref,
    scale_ref,
    gate_ref,
    qg_ref,
    kg_ref,
    kv_hbm,
    mask_ref,
    out_ref,
    xg,
    wq,
    wo,
    kvb,
    keys,
    vals,
    normed,
    queries,
    mixed,
    part,
    from_left,
    from_right,
    acc,
    local_sem,
    ag_send,
    ag_recv,
    rs_send,
    rs_left,
    rs_right,
    sec_send,
    sec_recv,
):
    me = lax.axis_index("tp")
    sec = lax.axis_index("section")
    after, before = lax.rem(sec + 1, sections), lax.rem(sec + sections - 1, sections)
    rows_all, share = x_ref.shape
    width = n * share
    tokens = kvb.shape[0]
    head_cols = wo.shape[0]
    size = rows_all // CHUNKS

    load_kv = pltpu.make_async_copy(kv_hbm, kvb, local_sem.at[0])
    load_wq = pltpu.make_async_copy(wq_hbm, wq, local_sem.at[1])
    load_wo = pltpu.make_async_copy(wo_hbm, wo, local_sem.at[2])
    load_kv.start()
    load_wq.start()
    load_wo.start()

    barrier = pltpu.get_barrier_semaphore()
    pl.semaphore_signal(barrier, inc=1, device_id={"section": after}, device_id_type=MESH)
    pl.semaphore_signal(barrier, inc=1, device_id={"section": before}, device_id_type=MESH)

    @pl.when(me > 0)
    def _():
        pl.semaphore_signal(barrier, inc=1, device_id={"tp": me - 1}, device_id_type=MESH)

    @pl.when(me < n - 1)
    def _():
        pl.semaphore_signal(barrier, inc=1, device_id={"tp": me + 1}, device_id_type=MESH)

    pl.semaphore_wait(barrier, 2 + jnp.minimum(me, 1) + jnp.minimum(n - 1 - me, 1))

    def rows(c):
        return pl.ds(c * size, size)

    def ag_copy(tick, way, step, c):
        shard = me - step if way == 0 else me + step
        here = xg.at[tick, shard, rows(c)]
        source = x_ref.at[rows(c)] if tick == 0 and step == 0 else here
        return pltpu.make_async_remote_copy(
            src_ref=source,
            dst_ref=here,
            send_sem=ag_send.at[tick, way, step, c],
            recv_sem=ag_recv.at[tick, shard, c],
            device_id={"tp": me + 1 if way == 0 else me - 1},
            device_id_type=MESH,
        )

    def ag_when(way, step):
        held = me - step >= 0 if way == 0 else me + step <= n - 1
        onward = me < n - 1 if way == 0 else me > 0
        return held, onward

    def ag_own(tick, c):
        for way in range(2):
            _, onward = ag_when(way, 0)

            @pl.when(onward)
            def _():
                ag_copy(tick, way, 0, c).start()

    def ag_relay(tick, c, step):
        for way in range(2):
            held, onward = ag_when(way, step)

            @pl.when(held)
            def _():
                ag_copy(tick, way, step, c).wait_recv()

                @pl.when(onward)
                def _():
                    ag_copy(tick, way, step, c).start()

    def ag_drain(tick, c):
        for step in range(n - 1):
            for way in range(2):
                held, onward = ag_when(way, step)

                @pl.when(held & onward)
                def _():
                    ag_copy(tick, way, step, c).wait_send()

    def rs_copy(tick, way, shard, c):
        landing, sems = (from_left, rs_left) if way == 0 else (from_right, rs_right)
        return pltpu.make_async_remote_copy(
            src_ref=part.at[shard, rows(c)],
            dst_ref=landing.at[tick, shard, rows(c)],
            send_sem=rs_send.at[tick, shard, c],
            recv_sem=sems.at[tick, shard, c],
            device_id={"tp": me + 1 if way == 0 else me - 1},
            device_id_type=MESH,
        )

    def rs_first(tick, c):
        @pl.when(me == 0)
        def _():
            for shard in range(n - 1, 0, -1):
                rs_copy(tick, 0, shard, c).start()

        @pl.when(me == n - 1)
        def _():
            for shard in range(n - 1):
                rs_copy(tick, 1, shard, c).start()

    def rs_rest(tick, c):
        for away in range(n - 1):
            far, near = n - 1 - away, away

            @pl.when((me > 0) & (me < far))
            def _():
                rs_copy(tick, 0, far, c).wait_recv()
                part[far, rows(c)] = (
                    part[far, rows(c)].astype(F32) + from_left[tick, far, rows(c)].astype(F32)
                ).astype(BF16)
                rs_copy(tick, 0, far, c).start()

            @pl.when((me < n - 1) & (me > near))
            def _():
                rs_copy(tick, 1, near, c).wait_recv()
                part[near, rows(c)] = (
                    part[near, rows(c)].astype(F32) + from_right[tick, near, rows(c)].astype(F32)
                ).astype(BF16)
                rs_copy(tick, 1, near, c).start()

    def rs_drain(tick, c):
        for shard in range(n):
            for way in range(2):
                going = me < shard if way == 0 else me > shard

                @pl.when(going)
                def _():
                    rs_copy(tick, way, shard, c).wait_send()

    def sec_copy(c):
        return pltpu.make_async_remote_copy(
            src_ref=out_ref.at[rows(c)],
            dst_ref=xg.at[1, me, rows(c)],
            send_sem=sec_send.at[c],
            recv_sem=sec_recv.at[c],
            device_id={"section": after},
            device_id_type=MESH,
        )

    def finish(tick, c):
        acc[...] = part[me, rows(c)].astype(F32)

        @pl.when(me > 0)
        def _():
            rs_copy(tick, 0, me, c).wait_recv()
            acc[...] += from_left[tick, me, rows(c)].astype(F32)

        @pl.when(me < n - 1)
        def _():
            rs_copy(tick, 1, me, c).wait_recv()
            acc[...] += from_right[tick, me, rows(c)].astype(F32)

        if tick + 1 == TICKS:
            sec_copy(c).wait_send()
        state = xg[tick, me, rows(c)].astype(F32)
        out_ref[rows(c), :] = (state + gate_ref[me] * acc[...]).astype(BF16)
        if tick + 1 < TICKS:
            sec_copy(c).start()

    def project(tick, c):
        def total(j, sums):
            return sums + jnp.sum(xg[tick, j, rows(c)].astype(F32), axis=-1, keepdims=True)

        center = lax.fori_loop(0, n, total, jnp.zeros((size, 1), F32)) / width

        def spread(j, sums):
            off = xg[tick, j, rows(c)].astype(F32) - center
            return sums + jnp.sum(off * off, axis=-1, keepdims=True)

        varied = lax.fori_loop(0, n, spread, jnp.zeros((size, 1), F32)) / width
        inverse = lax.rsqrt(varied + 1e-06)

        @pl.loop(0, n)
        def _(j):
            off = xg[tick, j, rows(c)].astype(F32) - center
            normed[:, pl.ds(pl.multiple_of(j * share, 128), share)] = (
                off * inverse * (1.0 + scale_ref[j]) + shift_ref[j]
            ).astype(BF16)

        at = pl.ds(tokens + tick * rows_all + c * size, size)

        @pl.loop(0, head_cols // 256)
        def _(h):
            start = pl.multiple_of(h * 256, 256)
            cols = pl.ds(start, 256)
            for kind in range(3):
                fresh = jnp.dot(normed[...], wq[kind, :, cols], preferred_element_type=F32).astype(BF16)
                if kind == 2:
                    vals[at, cols] = fresh
                    continue
                for half in range(2):
                    head = fresh[:, half * HD : (half + 1) * HD].astype(F32)
                    head_at = pl.ds(pl.multiple_of(start + half * HD, HD), HD)
                    if kind == 0:
                        queries[rows(c), head_at] = head_norm(head, qg_ref[...])
                    else:
                        keys[at, head_at] = head_norm(head, kg_ref[...])

    def attend(tick, c):
        count = tokens + (tick + 1) * rows_all

        @pl.loop(0, head_cols // HD)
        def _(h):
            cols = pl.ds(pl.multiple_of(h * HD, HD), HD)
            scores = lax.dot_general(
                queries[rows(c), cols],
                keys[0:count, cols],
                (((1,), (1,)), ((), ())),
                preferred_element_type=F32,
            )
            expon = jnp.exp(scores * HD ** (-0.5)) * mask_ref[tick : tick + 1, 0:count]
            total = jnp.sum(expon, axis=-1, keepdims=True)
            probs = (expon * (1.0 / total)).astype(BF16)
            mixed[:, cols] = jnp.dot(
                probs, vals[0:count, cols], preferred_element_type=F32
            ).astype(BF16)

        @pl.loop(0, n)
        def _(j):
            cols = pl.ds(pl.multiple_of(j * share, 128), share)
            part[j, rows(c)] = jnp.dot(
                mixed[...], wo[:, cols], preferred_element_type=F32
            ).astype(BF16)

    for c in range(CHUNKS):
        ag_own(0, c)
    xg[0, me] = x_ref[...]

    load_kv.wait()
    block = 128

    @pl.loop(0, tokens // block)
    def _(i):
        at = pl.ds(pl.multiple_of(i * block, block), block)
        raw = kvb[at]
        vals[at, :] = raw[:, 1, :]
        cached = raw[:, 0, :].astype(F32)
        for h in range(head_cols // HD):
            cols = slice(h * HD, (h + 1) * HD)
            keys[at, cols] = head_norm(cached[:, cols], kg_ref[...])

    for step in range(1, n):
        for c in range(CHUNKS):
            ag_relay(0, c, step)
            if step == n - 1:
                if c == 0:
                    load_wq.wait()
                    load_wo.wait()
                if c > 0:
                    project(0, c - 1)
    project(0, CHUNKS - 1)

    for i in range(CHUNKS + 4):
        if i < CHUNKS:
            attend(0, i)
            rs_first(0, i)
        if 0 <= i - 1 < CHUNKS:
            rs_rest(0, i - 1)
            finish(0, i - 1)
        if 0 <= i - 2 < CHUNKS:
            sec_copy(i - 2).wait_recv()
            ag_own(1, i - 2)
        if 0 <= i - 3 < CHUNKS:
            for step in range(1, n):
                ag_relay(1, i - 3, step)
        if 0 <= i - 4 < CHUNKS:
            project(1, i - 4)
    for c in range(CHUNKS):
        rs_drain(0, c)
    for i in range(CHUNKS + 1):
        if i < CHUNKS:
            attend(1, i)
            rs_first(1, i)
        if 0 <= i - 1 < CHUNKS:
            rs_rest(1, i - 1)
            finish(1, i - 1)
    for c in range(CHUNKS):
        ag_drain(0, c)
        ag_drain(1, c)
        rs_drain(1, c)


def local(
    inflow,
    w_qkv,
    w_out,
    mod_shift,
    mod_scale,
    mod_gate,
    q_gain,
    k_gain,
    kv_cache,
    patch_id,
    positions,
):
    n = lax.axis_size("tp")
    sections = lax.axis_size("section")
    section_no = lax.axis_index("section")
    width = w_out.shape[2]
    head_cols = w_out.shape[1]
    tokens = kv_cache.shape[1]
    patch_rows, share = inflow.shape[1:]
    span = tokens + TICKS * patch_rows
    token_line = jnp.arange(tokens, dtype=jnp.int32)
    mine = lax.dynamic_index_in_dim(patch_id, section_no, 1, keepdims=False)
    rows_at = jnp.take(positions, mine, axis=0)
    hit = jnp.any(rows_at[:, :, None] == token_line[None, None, :], axis=1)
    kept = 1.0 - hit.astype(jnp.float32)
    kept = jnp.concatenate([kept[0:1], kept[0:1] * kept[1:2]], axis=0)
    mask = jnp.concatenate([kept, jnp.ones((TICKS, span - tokens), jnp.float32)], axis=1)
    vmem = pl.BlockSpec(memory_space=pltpu.VMEM)
    hbm = pl.BlockSpec(memory_space=pl.ANY)
    size = patch_rows // CHUNKS
    dma = pltpu.SemaphoreType.DMA
    flops = 2 * TICKS * patch_rows * (4 * width * head_cols + 2 * span * head_cols)
    result = pl.pallas_call(
        functools.partial(kernel, n, sections),
        out_shape=jax.ShapeDtypeStruct((patch_rows, share), BF16),
        in_specs=[vmem, hbm, hbm, vmem, vmem, vmem, vmem, vmem, hbm, vmem],
        out_specs=vmem,
        scratch_shapes=[
            pltpu.VMEM((TICKS, n, patch_rows, share), BF16),
            pltpu.VMEM((3, width, head_cols), BF16),
            pltpu.VMEM((head_cols, width), BF16),
            pltpu.VMEM((tokens, 2, head_cols), BF16),
            pltpu.VMEM((span, head_cols), BF16),
            pltpu.VMEM((span, head_cols), BF16),
            pltpu.VMEM((size, width), BF16),
            pltpu.VMEM((patch_rows, head_cols), BF16),
            pltpu.VMEM((size, head_cols), BF16),
            pltpu.VMEM((n, patch_rows, share), BF16),
            pltpu.VMEM((TICKS, n, patch_rows, share), BF16),
            pltpu.VMEM((TICKS, n, patch_rows, share), BF16),
            pltpu.VMEM((size, share), F32),
            dma((3,)),
            dma((TICKS, 2, n, CHUNKS)),
            dma((TICKS, n, CHUNKS)),
            dma((TICKS, n, CHUNKS)),
            dma((TICKS, n, CHUNKS)),
            dma((TICKS, n, CHUNKS)),
            dma((CHUNKS,)),
            dma((CHUNKS,)),
        ],
        compiler_params=pltpu.CompilerParams(
            collective_id=0, has_side_effects=True, vmem_limit_bytes=56 * 1024 * 1024
        ),
        cost_estimate=pl.CostEstimate(
            flops=flops, bytes_accessed=16 * 1024 * 1024, transcendentals=4 * patch_rows * span
        ),
    )(
        inflow[0],
        jnp.transpose(w_qkv[0], (1, 0, 2)),
        w_out[0],
        mod_shift.reshape(n, 1, share),
        mod_scale.reshape(n, 1, share),
        mod_gate.reshape(n, 1, share),
        q_gain,
        k_gain,
        kv_cache[0],
        mask,
    )
    return result[None]


def solution(mesh):
    placed = (
        P("section", "cfg", "tp"),
        P("section", None, None, "tp"),
        P("section", "tp", None),
        P("section", None),
        P("section", None),
        P("section", None),
        P("section", None),
        P("section", None),
        P("section", "cfg", None, "tp"),
        P(),
        P(),
    )
    return jax.shard_map(
        local, mesh=mesh, in_specs=placed, out_specs=P("section", "cfg", "tp"), check_vma=False
    )
```

time: 257 us -> 189 us (0.74)
  Pallas kernels: 0 us -> 184 us
  waiting for transfers between devices: 158 us -> 0 us
  matrix products: 25.9 us -> 0 us
  local copies, waits for them, and re-layouts: 27.4 us -> 2.33 us
  other arithmetic: 26.5 us -> 2.86 us
  between operations: 17.3 us -> 0.04 us
    pallas_call x0 -> x1, Pallas kernels: none -> 184 us  [local(): pl.pallas_call(functools.partial(kernel, n, sections), out_shape=jax.Shap...]
    psum x2 -> x0, waiting for transfers between devices: 133 us -> none  [local(): lax.psum(partial_value.astype(jnp.bfloat16), 'tp').astype(jnp.float32)]
    dot_general x14 -> x0, matrix products: 25.9 us -> none  [the longest x2 14.6 us: local(): fresh = jnp.dot(normed, weight_in, preferred_element_type=jnp.float32)]
    ppermute x1 -> x0, waiting for transfers between devices: 19.8 us -> none  [passed_along(): return lax.ppermute(value, axis, pairs)]
    convert_element_type x4 -> x0, other arithmetic: 16 us -> none  [the longest x1 6.92 us: local(): cache_raw[:, 0].astype(jnp.float32).reshape(tokens_all, head_count, HD)]
    unnamed x35 -> x3, local copies, waits for them, and re-layouts: 13.7 us -> 1.77 us
    slice x4 -> x0, local copies, waits for them, and re-layouts: 8.36 us -> none  [the longest x1 5.86 us: local(): cache_vals = cache_raw[:, 1].reshape(tokens_all, head_count, HD)]
    reduce_sum x9 -> x0, other arithmetic: 7.8 us -> none  [the longest x5 3.18 us: rms_scale(): moment = jnp.mean(values * values, axis=-1, keepdims=True)]
  transfers between devices with their start and end apart: 4 -> 0, of which waited for: 4 -> 0; matrix products, arithmetic and copies ran while one was open for 14% -> 0% of each run, Pallas kernels for 0% -> 0%
where the time goes in v1:
time: 189 us
  Pallas kernels  184 us (97%)
  other arithmetic  2.86 us (2%)
  local copies, waits for them, and re-layouts  2.33 us (1%)
    pallas_call x1, Pallas kernels, local(): pl.pallas_call(functools.partial(kernel, n, sections), out_shape=jax.Shap...  184 us

profile of v1, /device:TPU:0, one launch (start us, length us, event | category | flops | bytes accessed | tf_op | source)
XLA Modules:
  0.0 188.9 jit_solution(1616594734330676391)
XLA Ops:
  0.0 0.0 copy-start
  0.0 0.9 and_reduce_fusion
  0.9 0.9 fusion.1
  1.8 0.0 copy-done
  1.8 0.6 gather_fusion
  2.3 0.1 broadcast_select_fusion
  2.4 0.4 fusion
  2.8 0.6 select_maximum_fusion.mask_ref
  3.4 183.7 %shard_map.109 = bf16[256,768]{1,0:T(8,128)(2,1)} custom-call(bf16[256,768]{1,0:T(8,128)(2,1)} %bitcast.14, bf16[3,3072,512]{2,1,0:T(8,128)(2,1)} %bitcast.11, bf16[512,3072]{1,0:T(8,128)(2,1)} %bitcast.12, f32[4,1,768]{2,1,0:T(1,128)} %bitcast.15, f32[4,1,768]{2,1,0:T(1,128)} %bitcast.16, f32[4,1,768]{2,1,0:T(1,128)} %bitcast.17, f32[1,128]{1,0:T(1,128)} %qg_ref.1, ...), custom_call_target="tpu_custom_call" | custom-call | flops 8053063680 | bytes 16777216 | tf_op jit(solution)/shard_map/pallas_call | solution.py:376
  187.2 1.8 copy.13
  (3 shorter events, 0.0 us)
Async XLA Ops:
  0.0 1.8 copy-start

commit v2 on v1

--- a/solution.py
+++ b/solution.py
@@ -9,7 +9,7 @@
 
 HD = 128
 TICKS = 2
-CHUNKS = 4
+CHUNKS = 2
 MESH = pl.DeviceIdType.MESH
 F32 = jnp.float32
 BF16 = jnp.bfloat16
@@ -310,30 +310,31 @@
                     project(0, c - 1)
     project(0, CHUNKS - 1)
 
-    for i in range(CHUNKS + 4):
-        if i < CHUNKS:
-            attend(0, i)
-            rs_first(0, i)
-        if 0 <= i - 1 < CHUNKS:
-            rs_rest(0, i - 1)
-            finish(0, i - 1)
-        if 0 <= i - 2 < CHUNKS:
-            sec_copy(i - 2).wait_recv()
-            ag_own(1, i - 2)
-        if 0 <= i - 3 < CHUNKS:
-            for step in range(1, n):
-                ag_relay(1, i - 3, step)
-        if 0 <= i - 4 < CHUNKS:
-            project(1, i - 4)
+    for c in range(CHUNKS):
+        attend(0, c)
+        rs_first(0, c)
+    for c in range(CHUNKS):
+        rs_rest(0, c)
+    for c in range(CHUNKS):
+        finish(0, c)
+    for c in range(CHUNKS):
+        sec_copy(c).wait_recv()
+        ag_own(1, c)
+    for step in range(1, n):
+        for c in range(CHUNKS):
+            ag_relay(1, c, step)
+            if step == n - 1 and c > 0:
+                project(1, c - 1)
+    project(1, CHUNKS - 1)
     for c in range(CHUNKS):
         rs_drain(0, c)
-    for i in range(CHUNKS + 1):
-        if i < CHUNKS:
-            attend(1, i)
-            rs_first(1, i)
-        if 0 <= i - 1 < CHUNKS:
-            rs_rest(1, i - 1)
-            finish(1, i - 1)
+    for c in range(CHUNKS):
+        attend(1, c)
+        rs_first(1, c)
+    for c in range(CHUNKS):
+        rs_rest(1, c)
+    for c in range(CHUNKS):
+        finish(1, c)
     for c in range(CHUNKS):
         ag_drain(0, c)
         ag_drain(1, c)

time: 189 us -> 154 us (0.81)
  Pallas kernels: 184 us -> 148 us
    pallas_call x1, Pallas kernels: 184 us -> 148 us  [local(): pl.pallas_call(functools.partial(kernel, n, sections), out_shape=jax.Shap...]
where the time goes in v2:
time: 154 us; the launch traced here: 153 us
  Pallas kernels  148 us (96%)
  other arithmetic  2.86 us (2%)
  local copies, waits for them, and re-layouts  2.33 us (2%)
    pallas_call x1, Pallas kernels, local(): pl.pallas_call(functools.partial(kernel, n, sections), out_shape=jax.Shap...  148 us

profile of v2, /device:TPU:0, one launch (start us, length us, event | category | flops | bytes accessed | tf_op | source)
XLA Modules:
  0.0 153.4 jit_solution(17018106063967062917)
XLA Ops:
  0.0 0.0 copy-start
  0.0 0.9 and_reduce_fusion
  0.9 0.9 fusion.1
  1.8 0.0 copy-done
  1.8 0.6 gather_fusion
  2.3 0.1 broadcast_select_fusion
  2.4 0.4 fusion
  2.8 0.6 select_maximum_fusion.mask_ref
  3.4 148.1 %shard_map.109 = bf16[256,768]{1,0:T(8,128)(2,1)} custom-call(bf16[256,768]{1,0:T(8,128)(2,1)} %bitcast.14, bf16[3,3072,512]{2,1,0:T(8,128)(2,1)} %bitcast.11, bf16[512,3072]{1,0:T(8,128)(2,1)} %bitcast.12, f32[4,1,768]{2,1,0:T(1,128)} %bitcast.15, f32[4,1,768]{2,1,0:T(1,128)} %bitcast.16, f32[4,1,768]{2,1,0:T(1,128)} %bitcast.17, f32[1,128]{1,0:T(1,128)} %qg_ref.1, ...), custom_call_target="tpu_custom_call" | custom-call | flops 8053063680 | bytes 16777216 | tf_op jit(solution)/shard_map/pallas_call | solution.py:377
  151.6 1.8 %copy.13 = bf16[1,256,768]{2,1,0:T(8,128)(2,1)} copy(bf16[1,256,768]{2,1,0:T(8,128)(2,1)} %bitcast.10) | data formatting | bytes 786432
  (3 shorter events, 0.0 us)
Async XLA Ops:
  0.0 1.8 %copy-start = (s32[4,256]{1,0:T(4,128)S(1)}, s32[4,256]{1,0:T(4,128)}, u32[]{:S(2)}) copy-start(s32[4,256]{1,0:T(4,128)} %param.21) | copy-start | bytes 12292

commit v3 on v2

--- a/solution.py
+++ b/solution.py
@@ -217,27 +217,27 @@
         if tick + 1 < TICKS:
             sec_copy(c).start()
 
-    def project(tick, c):
+    def project(tick):
         def total(j, sums):
-            return sums + jnp.sum(xg[tick, j, rows(c)].astype(F32), axis=-1, keepdims=True)
-
-        center = lax.fori_loop(0, n, total, jnp.zeros((size, 1), F32)) / width
+            return sums + jnp.sum(xg[tick, j, pl.ds(0, rows_all)].astype(F32), axis=-1, keepdims=True)
+
+        center = lax.fori_loop(0, n, total, jnp.zeros((rows_all, 1), F32)) / width
 
         def spread(j, sums):
-            off = xg[tick, j, rows(c)].astype(F32) - center
+            off = xg[tick, j, pl.ds(0, rows_all)].astype(F32) - center
             return sums + jnp.sum(off * off, axis=-1, keepdims=True)
 
-        varied = lax.fori_loop(0, n, spread, jnp.zeros((size, 1), F32)) / width
+        varied = lax.fori_loop(0, n, spread, jnp.zeros((rows_all, 1), F32)) / width
         inverse = lax.rsqrt(varied + 1e-06)
 
         @pl.loop(0, n)
         def _(j):
-            off = xg[tick, j, rows(c)].astype(F32) - center
+            off = xg[tick, j, pl.ds(0, rows_all)].astype(F32) - center
             normed[:, pl.ds(pl.multiple_of(j * share, 128), share)] = (
                 off * inverse * (1.0 + scale_ref[j]) + shift_ref[j]
             ).astype(BF16)
 
-        at = pl.ds(tokens + tick * rows_all + c * size, size)
+        at = pl.ds(tokens + tick * rows_all, rows_all)
 
         @pl.loop(0, head_cols // 256)
         def _(h):
@@ -252,7 +252,7 @@
                     head = fresh[:, half * HD : (half + 1) * HD].astype(F32)
                     head_at = pl.ds(pl.multiple_of(start + half * HD, HD), HD)
                     if kind == 0:
-                        queries[rows(c), head_at] = head_norm(head, qg_ref[...])
+                        queries[pl.ds(0, rows_all), head_at] = head_norm(head, qg_ref[...])
                     else:
                         keys[at, head_at] = head_norm(head, kg_ref[...])
 
@@ -306,9 +306,7 @@
                 if c == 0:
                     load_wq.wait()
                     load_wo.wait()
-                if c > 0:
-                    project(0, c - 1)
-    project(0, CHUNKS - 1)
+    project(0)
 
     for c in range(CHUNKS):
         attend(0, c)
@@ -323,9 +321,7 @@
     for step in range(1, n):
         for c in range(CHUNKS):
             ag_relay(1, c, step)
-            if step == n - 1 and c > 0:
-                project(1, c - 1)
-    project(1, CHUNKS - 1)
+    project(1)
     for c in range(CHUNKS):
         rs_drain(0, c)
     for c in range(CHUNKS):
@@ -386,7 +382,7 @@
             pltpu.VMEM((tokens, 2, head_cols), BF16),
             pltpu.VMEM((span, head_cols), BF16),
             pltpu.VMEM((span, head_cols), BF16),
-            pltpu.VMEM((size, width), BF16),
+            pltpu.VMEM((patch_rows, width), BF16),
             pltpu.VMEM((patch_rows, head_cols), BF16),
             pltpu.VMEM((size, head_cols), BF16),
             pltpu.VMEM((n, patch_rows, share), BF16),

time: 154 us -> 151 us (0.981)
  Pallas kernels: 148 us -> 146 us
    pallas_call x1, Pallas kernels: 148 us -> 146 us  [local(): pl.pallas_call(functools.partial(kernel, n, sections), out_shape=jax.Shap...]
where the time goes in v3:
time: 151 us
  Pallas kernels  146 us (97%)
  other arithmetic  2.86 us (2%)
  local copies, waits for them, and re-layouts  2.33 us (2%)
    pallas_call x1, Pallas kernels, local(): pl.pallas_call(functools.partial(kernel, n, sections), out_shape=jax.Shap...  146 us

profile of v3, /device:TPU:0, one launch (start us, length us, event | category | flops | bytes accessed | tf_op | source)
XLA Modules:
  0.0 151.0 jit_solution(4790051332566406177)
XLA Ops:
  0.0 0.0 copy-start
  0.0 0.9 and_reduce_fusion
  0.9 0.9 fusion.1
  1.8 0.0 copy-done
  1.8 0.6 gather_fusion
  2.3 0.1 broadcast_select_fusion
  2.4 0.4 fusion
  2.8 0.6 select_maximum_fusion.mask_ref
  3.4 145.8 %shard_map.109 = bf16[256,768]{1,0:T(8,128)(2,1)} custom-call(bf16[256,768]{1,0:T(8,128)(2,1)} %bitcast.14, bf16[3,3072,512]{2,1,0:T(8,128)(2,1)} %bitcast.11, bf16[512,3072]{1,0:T(8,128)(2,1)} %bitcast.12, f32[4,1,768]{2,1,0:T(1,128)} %bitcast.15, f32[4,1,768]{2,1,0:T(1,128)} %bitcast.16, f32[4,1,768]{2,1,0:T(1,128)} %bitcast.17, f32[1,128]{1,0:T(1,128)} %qg_ref.1, ...), custom_call_target="tpu_custom_call" | custom-call | flops 8053063680 | bytes 16777216 | tf_op jit(solution)/shard_map/pallas_call | solution.py:373
  149.2 1.8 %copy.13 = bf16[1,256,768]{2,1,0:T(8,128)(2,1)} copy(bf16[1,256,768]{2,1,0:T(8,128)(2,1)} %bitcast.10) | data formatting | bytes 786432
  (3 shorter events, 0.0 us)
Async XLA Ops:
  0.0 1.8 %copy-start = (s32[4,256]{1,0:T(4,128)S(1)}, s32[4,256]{1,0:T(4,128)}, u32[]{:S(2)}) copy-start(s32[4,256]{1,0:T(4,128)} %param.21) | copy-start | bytes 12292
